TPU v7x, 32 devices: a whole 2x2x4 slice. The times are simulated.
32 devices in a mesh: segment: 2 (over core), expert: 16 (over z, y, x).
Axes of the slice: x: 2, y: 2, z: 4, core: 2. Of those that a mesh axis runs over, the one named last changes fastest.
Arguments:
- tokens: bfloat16 [2, 1024, 2048], P(None, 'expert'), may hold values from -6 to 6
- routing: int32 [2, 2, 1024, 8], P(None, None, 'expert'), may hold values from 0 to 15, all different within a row; in each aligned block of 64 rows (0 to 63, 64 to 127, ..., all dimensions but the last counted through in order) at most 64 rows name the same one
- norm_gain: bfloat16 [2, 2048], P('segment'), may hold values from 0.5 to 1.5
- router_weight: bfloat16 [2, 2048, 16], P('segment'), may hold values from -0.125 to 0.125
- expert_gate_up: bfloat16 [2, 16, 2048, 768], P('segment', 'expert'), may hold values from -0.125 to 0.125
- expert_down: bfloat16 [2, 16, 384, 2048], P('segment', 'expert'), may hold values from -0.3125 to 0.3125
- pair_index: int32 [64], replicated, may hold values from 0 to 63, each once
- topic_ids: int32 [64], replicated, may hold values from 0 to 7
Outputs:
- final_hidden: bfloat16 [2, 1024, 2048], P('segment', 'expert')
- query_loss: float32 [64], P(('segment', 'expert'))
Inputs may be any that keep to these rules, and one draw needn't show every extreme that they name: `routing`: each row names 8 different experts. In the rows of one device (each aligned block of 64 token rows of one layer and micro-batch) no expert is named by more than 64 rows, a bound that some block reaches. `pair_index`: every passage is the positive of exactly one query.
All inputs are finite; a program needn't handle non-finite values.
Results may differ from a plain program's by a relative error of at most 0.0059.
Values may be sent and summed in bfloat16 or wider, within the bound.
A program may use at most 128 MiB of HBM per device.

v0:
```python
import jax
import jax.numpy as jnp
from jax import lax
from jax.sharding import PartitionSpec as P

SEQ = 16
EPSILON = 1e-06
SOFTMAX_WARMTH = 0.05


def passed_along(block, axis, distance):
    devices = range(lax.axis_size(axis))
    route = [(i - distance, i) for i in devices if i - distance in devices]
    return lax.ppermute(block, axis, route)


def expert_block(received, gate_up, down_proj):
    source_count, slot_count, model_width = received.shape
    flat_rows = received.reshape(source_count * slot_count, model_width)
    projected = jnp.dot(flat_rows, gate_up, preferred_element_type=jnp.float32)
    half_width = gate_up.shape[1] // 2
    hidden = (jax.nn.silu(projected[:, :half_width]) * projected[:, half_width:]).astype(
        jnp.bfloat16
    )
    result = jnp.dot(hidden, down_proj, preferred_element_type=jnp.float32).astype(jnp.bfloat16)
    return result.reshape(source_count, slot_count, model_width)


def moe_layer(inputs, routes, norm_gain, router_weight, gate_up, down_proj):
    row_count, model_width = inputs.shape
    top_count = routes.shape[1]
    expert_count = router_weight.shape[1]
    capacity = 2 * row_count * top_count // expert_count
    widened = inputs.astype(jnp.float32)
    normed = (
        widened
        * lax.rsqrt(jnp.mean(widened * widened, axis=1, keepdims=True) + EPSILON)
        * norm_gain.astype(jnp.float32)
    ).astype(jnp.bfloat16)
    similarity_logits = jnp.dot(normed, router_weight, preferred_element_type=jnp.float32)
    chosen = jnp.take_along_axis(similarity_logits, routes, axis=1)
    raised = jnp.exp(chosen)
    gate_weights = raised / jnp.sum(raised, axis=1, keepdims=True)
    flat_ids = routes.reshape(-1)
    one_hot = (flat_ids[:, None] == jnp.arange(expert_count, dtype=jnp.int32)[None, :]).astype(
        jnp.int32
    )
    earlier = jnp.cumsum(one_hot, axis=0) - one_hot
    slot_index = jnp.sum(earlier * one_hot, axis=1)
    target = flat_ids * capacity + slot_index
    repeated = jnp.repeat(normed, top_count, axis=0)
    outgoing = (
        jnp.zeros((expert_count * capacity, model_width), jnp.bfloat16).at[target].set(repeated)
    )
    outgoing = outgoing.reshape(expert_count, capacity, model_width)
    answered = expert_block(
        lax.all_to_all(outgoing, "expert", split_axis=0, concat_axis=0, tiled=True),
        gate_up,
        down_proj,
    )
    returned = lax.all_to_all(answered, "expert", split_axis=0, concat_axis=0, tiled=True)
    picked = returned.reshape(expert_count * capacity, model_width)[target].astype(jnp.float32)
    picked = picked.reshape(row_count, top_count, model_width)
    mixture = jnp.sum(picked * gate_weights[:, :, None], axis=1)
    return (widened + mixture).astype(jnp.bfloat16)


def pooled_embeddings(final_rows):
    widened = final_rows.astype(jnp.float32)
    pooled = jnp.mean(widened.reshape(-1, SEQ, widened.shape[1]), axis=1)
    return (pooled * lax.rsqrt(jnp.sum(pooled * pooled, axis=1, keepdims=True) + EPSILON)).astype(
        jnp.bfloat16
    )


def local(
    tokens, routing, norm_gain, router_weight, expert_gate_up, expert_down, pair_index, topic_ids
):
    segment_index = lax.axis_index("segment")
    micro_count = tokens.shape[0]
    segment_routes = lax.dynamic_index_in_dim(routing, segment_index, 0, keepdims=False)
    carried = jnp.zeros_like(tokens[0])
    finished = []
    for time_step in range(micro_count + 1):
        fresh_rows = tokens[min(time_step, micro_count - 1)]
        segment_input = jnp.where(segment_index == 0, fresh_rows, carried)
        micro_pick = jnp.clip(time_step - segment_index, 0, micro_count - 1)
        layer_routes = lax.dynamic_index_in_dim(segment_routes, micro_pick, 0, keepdims=False)
        produced = moe_layer(
            segment_input,
            layer_routes,
            norm_gain[0],
            router_weight[0],
            expert_gate_up[0, 0],
            expert_down[0, 0],
        )
        finished.append(produced)
        if time_step < micro_count:
            carried = passed_along(produced, "segment", 1)
    sent_back = passed_along(finished[1], "segment", -1)
    final_rows = jnp.where(segment_index == 0, sent_back, finished[micro_count])
    embedded = pooled_embeddings(final_rows)
    half_count = embedded.shape[0] // 2
    query_vectors = embedded[:half_count]
    passage_vectors = embedded[half_count:]
    device_flat = lax.axis_index(("segment", "expert"))
    columns = jnp.arange(topic_ids.shape[0], dtype=jnp.int32)
    matched = pair_index[:, None] == columns[None, :]
    positive_topic = jnp.sum(
        jnp.where(matched, topic_ids[None, :], jnp.zeros_like(topic_ids)[None, :]), axis=1
    )
    every_query_row = lax.all_gather(query_vectors, ("segment", "expert"), axis=0, tiled=True)
    local_ids = device_flat * half_count + jnp.arange(half_count, dtype=jnp.int32)
    local_topics = lax.dynamic_slice_in_dim(topic_ids, device_flat * half_count, half_count)
    pair_scores = (
        jnp.dot(every_query_row, passage_vectors.T, preferred_element_type=jnp.float32)
        / SOFTMAX_WARMTH
    )
    is_positive = pair_index[:, None] == local_ids[None, :]
    kept_pairs = is_positive | (local_topics[None, :] != positive_topic[:, None])
    partition_part = jnp.sum(
        jnp.where(kept_pairs, jnp.exp(pair_scores), jnp.zeros_like(pair_scores)), axis=1
    )
    positive_part = jnp.sum(
        jnp.where(is_positive, pair_scores, jnp.zeros_like(pair_scores)), axis=1
    )
    partition, positive = (
        lax.psum_scatter(partition_part, ("segment", "expert"), scatter_dimension=0, tiled=True),
        lax.psum_scatter(positive_part, ("segment", "expert"), scatter_dimension=0, tiled=True),
    )
    query_loss = jnp.log(partition) - positive
    return (final_rows[None], query_loss)


def solution(mesh):
    in_specs = (
        P(None, "expert", None),
        P(None, None, "expert", None),
        P("segment", None),
        P("segment", None, None),
        P("segment", "expert", None, None),
        P("segment", "expert", None, None),
        P(),
        P(),
    )
    out_specs = (P("segment", "expert", None), P(("segment", "expert")))
    return jax.shard_map(local, mesh=mesh, in_specs=in_specs, out_specs=out_specs, check_vma=False)
```

profile of v0, /device:TPU:14, one launch (start us, length us, event | category | flops | bytes accessed | tf_op | source)
XLA Modules:
  0.0 794.9 jit_solution(5908741902070264360)
XLA Ops:
  6.5 6.2 scatter_custom_fusion
  12.6 98.8 %all_to_all.30 = bf16[16,64,2048]{2,1,0:T(8,128)(2,1)S(1)} all-to-all(bf16[16,64,2048]{2,1,0:T(8,128)(2,1)} %bitcast.211), channel_id=1, replica_groups=mesh['segment'=2,'expert'=16] {'expert'}, dimensions={0} | all-to-all | bytes 8388608 | tf_op jit(solution)/shard_map/all_to_all | solution.py:57
  111.5 3.4 fusion.7
  114.9 4.3 convolution_convert_fusion.2
  119.2 7.0 all-to-all-start.1
  127.9 3.9 gather_fusion.3
  133.5 84.3 %all-to-all-done.1 = bf16[16,64,2048]{2,1,0:T(8,128)(2,1)} async-done(((bf16[16,64,2048]{2,1,0:T(8,128)(2,1)}), bf16[16,64,2048]{2,1,0:T(8,128)(2,1)}, u32[]{:S(2)}, u32[]{:S(2)}) %all-to-all-start.1) | async-done | bytes 4194336 | tf_op jit(solution)/shard_map/all_to_all | solution.py:61
  217.8 8.0 %gather_fusion = bf16[512,2048]{1,0:T(8,128)(2,1)} fusion(bf16[1024,2048]{1,0:T(8,128)(2,1)} %bitcast.12, s32[1024]{0:T(1024)S(1)} %pad_clamp_fusion.2), kind=kCustom, calls=%fused_computation.3 | custom fusion | bytes 4196352 | tf_op jit(solution)/shard_map/gather | solution.py:62
  225.8 3.4 fusion.2
  235.6 6.2 scatter_custom_fusion.1
  241.7 97.5 %all_to_all.31 = bf16[16,64,2048]{2,1,0:T(8,128)(2,1)S(1)} all-to-all(bf16[16,64,2048]{2,1,0:T(8,128)(2,1)} %bitcast.213), channel_id=1, replica_groups=mesh['segment'=2,'expert'=16] {'expert'}, dimensions={0} | all-to-all | bytes 8388608 | tf_op jit(solution)/shard_map/all_to_all | solution.py:57
  339.3 3.4 fusion.5
  342.7 4.3 convolution_convert_fusion.1
  347.1 6.3 all-to-all-start.3
  354.4 2.2 reduce-window.26
  357.1 3.9 gather_fusion.4
  361.9 83.8 %all-to-all-done.3 = bf16[16,64,2048]{2,1,0:T(8,128)(2,1)} async-done(((bf16[16,64,2048]{2,1,0:T(8,128)(2,1)}), bf16[16,64,2048]{2,1,0:T(8,128)(2,1)}, u32[]{:S(2)}, u32[]{:S(2)}) %all-to-all-start.3) | async-done | bytes 4194336 | tf_op jit(solution)/shard_map/all_to_all | solution.py:61
  445.7 8.0 %gather_fusion.1 = bf16[512,2048]{1,0:T(8,128)(2,1)} fusion(bf16[1024,2048]{1,0:T(8,128)(2,1)} %bitcast.25, s32[1024]{0:T(1024)S(1)} %pad_clamp_fusion.1), kind=kCustom, calls=%fused_computation.4 | custom fusion | bytes 4196352 | tf_op jit(solution)/shard_map/gather | solution.py:62
  453.7 3.4 fusion.1
  457.9 2.4 collective-permute-start.2
  462.7 6.6 scatter_custom_fusion.2
  469.3 97.4 %all_to_all.32 = bf16[16,64,2048]{2,1,0:T(8,128)(2,1)S(1)} all-to-all(bf16[16,64,2048]{2,1,0:T(8,128)(2,1)} %bitcast.212), channel_id=1, replica_groups=mesh['segment'=2,'expert'=16] {'expert'}, dimensions={0} | all-to-all | bytes 8388608 | tf_op jit(solution)/shard_map/all_to_all | solution.py:57
  566.7 3.4 fusion.3
  570.1 4.3 convolution_convert_fusion
  574.5 6.3 all-to-all-start.5
  583.9 3.9 gather_fusion.5
  588.1 85.2 %all-to-all-done.5 = bf16[16,64,2048]{2,1,0:T(8,128)(2,1)} async-done(((bf16[16,64,2048]{2,1,0:T(8,128)(2,1)}), bf16[16,64,2048]{2,1,0:T(8,128)(2,1)}, u32[]{:S(2)}, u32[]{:S(2)}) %all-to-all-start.5) | async-done | bytes 4194336 | tf_op jit(solution)/shard_map/all_to_all | solution.py:61
  673.3 8.0 %gather_fusion.2 = bf16[512,2048]{1,0:T(8,128)(2,1)} fusion(bf16[1024,2048]{1,0:T(8,128)(2,1)} %bitcast.36, s32[1024]{0:T(1024)S(1)} %pad_clamp_fusion), kind=kCustom, calls=%fused_computation.5 | custom fusion | bytes 4196352 | tf_op jit(solution)/shard_map/gather | solution.py:62
  681.3 3.4 fusion
  684.8 1.8 convert_reduce_fusion
  686.8 57.1 %all-gather = bf16[32,2,2048]{2,1,0:T(2,128)(2,1)S(1)} all-gather(bf16[1,2,2048]{2,1,0:T(2,128)(2,1)S(1)} %slice_bitcast_fusion), channel_id=1, replica_groups=mesh['segment'=2,'expert'=16] {'segment','expert'}, dimensions={0}, use_global_device_ids=true | all-gather | bytes 270336 | tf_op jit(solution)/shard_map/all_gather | solution.py:112
  745.8 48.3 %all-reduce.2 = (f32[64]{0:T(128)S(1)}, f32[64]{0:T(128)S(1)}) all-reduce(f32[64]{0:T(128)S(1)} %get-tuple-element.4, f32[64]{0:T(128)S(1)} %get-tuple-element.3), channel_id=3, replica_groups=mesh['segment'=2,'expert'=16] {'segment','expert'}, use_global_device_ids=true, to_apply=%region_27.29.clone | all-reduce | flops 128 | bytes 1024
  (113 shorter events, 27.0 us)
Async XLA Ops:
  0.6 110.8 %copy-start = (bf16[1,1,2048,768]{3,2,1,0:T(8,128)(2,1)S(1)}, bf16[1,1,2048,768]{3,2,1,0:T(8,128)(2,1)}, u32[]{:S(2)}) copy-start(bf16[1,1,2048,768]{3,2,1,0:T(8,128)(2,1)} %param.14) | copy-start | bytes 9437188
  111.5 3.4 copy-start.5
  119.2 7.4 copy-start.3
  119.2 98.5 %all-to-all-start.1 = ((bf16[16,64,2048]{2,1,0:T(8,128)(2,1)}), bf16[16,64,2048]{2,1,0:T(8,128)(2,1)}, u32[]{:S(2)}, u32[]{:S(2)}) async-start(bf16[16,64,2048]{2,1,0:T(8,128)(2,1)} %bitcast.215), calls=%async_computation.1 | async-start | bytes 8388608 | tf_op jit(solution)/shard_map/all_to_all | solution.py:61
  230.9 2.6 collective-permute-start
  234.7 0.7 copy-start.1
  339.3 3.4 copy-start.6
  347.1 98.6 %all-to-all-start.3 = ((bf16[16,64,2048]{2,1,0:T(8,128)(2,1)}), bf16[16,64,2048]{2,1,0:T(8,128)(2,1)}, u32[]{:S(2)}, u32[]{:S(2)}) async-start(bf16[16,64,2048]{2,1,0:T(8,128)(2,1)} %bitcast.216), calls=%async_computation.3 | async-start | bytes 8388608 | tf_op jit(solution)/shard_map/all_to_all | solution.py:61
  356.9 4.1 copy-start.4
  445.7 11.5 %copy-start.2 = (bf16[64,2048]{1,0:T(8,128)(2,1)S(1)}, bf16[64,2048]{1,0:T(8,128)(2,1)}, u32[]{:S(2)}) copy-start(bf16[64,2048]{1,0:T(8,128)(2,1)} %copy-done.1) | copy-start | bytes 786436
  453.7 6.6 slice-start
  457.9 2.8 collective-permute-start.2
  566.7 3.4 copy-start.7
  574.5 6.5 copy-start.8
  574.5 6.6 copy-start.9
  574.5 98.8 %all-to-all-start.5 = ((bf16[16,64,2048]{2,1,0:T(8,128)(2,1)}), bf16[16,64,2048]{2,1,0:T(8,128)(2,1)}, u32[]{:S(2)}, u32[]{:S(2)}) async-start(bf16[16,64,2048]{2,1,0:T(8,128)(2,1)} %bitcast.214), calls=%async_computation.5 | async-start | bytes 8388608 | tf_op jit(solution)/shard_map/all_to_all | solution.py:61
  581.3 103.5 %collective-permute-start.1 = (bf16[64,2048]{1,0:T(8,128)(2,1)}, bf16[64,2048]{1,0:T(8,128)(2,1)}, u32[]{:S(2)}, u32[]{:S(2)}) collective-permute-start(bf16[64,2048]{1,0:T(8,128)(2,1)} %fusion.45), channel_id=1, source_target_pairs={{16,0},{17,1},{18,2},{19,3},{20,4},{21,5},{22,6},{23,7},{24,8},{25... | collective-permute-start | bytes 786440 | tf_op jit(solution)/shard_map/ppermute | solution.py:14
where the time goes:
time: 804 us; the launch traced here: 795 us
  blocking collectives  399 us (50%)
  waiting for transfers between devices  254 us (32%)
  local copies, waits for them, and re-layouts  60.1 us (7%)
  other arithmetic  28.4 us (4%)
  matrix products  26.9 us (3%)
  starting transfers between devices  24.7 us (3%)
    all_to_all x3, blocking collectives, moe_layer(): lax.all_to_all(outgoing, 'expert', split_axis=0, concat_axis=0, tiled=True)  294 us
    all_to_all x3, waiting for transfers between devices, moe_layer(): lax.all_to_all(answered, 'expert', split_axis=0, concat_axis=0, tiled=True)  253 us
    all_gather x1, blocking collectives, local(): lax.all_gather(query_vectors, ('segment', 'expert'), axis=0, tiled=True)  57.1 us
    unnamed x1, blocking collectives  48.3 us
    gather x3, local copies, waits for them, and re-layouts, moe_layer(): returned.reshape(expert_count * capacity, model_width)[target]  24 us
    all_to_all x3, starting transfers between devices, moe_layer(): lax.all_to_all(answered, 'expert', split_axis=0, concat_axis=0, tiled=True)  19.6 us
    scatter x3, local copies, waits for them, and re-layouts, moe_layer(): jnp.zeros((expert_count * capacity, model_width), jnp.bfloat16).at[target]  18.9 us
  transfers between devices with their start and end apart: 6, of which 5 were waited for; matrix products, arithmetic and copies ran while one was open for 4% of the time, Pallas kernels for 0%

commit v1 on v0

--- a/solution.py
+++ b/solution.py
@@ -6,6 +6,29 @@
 SEQ = 16
 EPSILON = 1e-06
 SOFTMAX_WARMTH = 0.05
+
+
+def split_up(x, dim, count):
+    shape = x.shape
+    blocks = x.reshape(*shape[:dim], count, shape[dim] // count, *shape[dim + 1 :])
+    return jnp.moveaxis(blocks, dim, 0)
+
+
+def in_order(tiles, dim):
+    dims = list(tiles.shape[1:])
+    dims[dim] *= tiles.shape[0]
+    return jnp.moveaxis(tiles, 0, dim).reshape(dims)
+
+
+def pairwise_exchange(x, axis, split_dim, concat_dim):
+    peers, index = (lax.axis_size(axis), lax.axis_index(axis))
+    pieces = split_up(x, split_dim, peers)
+    gathered = [pieces[index]]
+    for hop in range(1, peers):
+        sent = pieces[index ^ hop]
+        gathered.append(lax.ppermute(sent, axis, [(i, i ^ hop) for i in range(peers)]))
+    pieces = jnp.stack(gathered)[index ^ jnp.arange(peers)]
+    return in_order(pieces, concat_dim)
 
 
 def passed_along(block, axis, distance):
@@ -58,7 +81,7 @@
         gate_up,
         down_proj,
     )
-    returned = lax.all_to_all(answered, "expert", split_axis=0, concat_axis=0, tiled=True)
+    returned = pairwise_exchange(answered, "expert", 0, 0)
     picked = returned.reshape(expert_count * capacity, model_width)[target].astype(jnp.float32)
     picked = picked.reshape(row_count, top_count, model_width)
     mixture = jnp.sum(picked * gate_weights[:, :, None], axis=1)

time: 804 us -> 876 us (1.090)
  blocking collectives: 399 us -> 105 us
  waiting for transfers between devices: 254 us -> 472 us
  starting transfers between devices: 24.7 us -> 113 us
  local copies, waits for them, and re-layouts: 60.1 us -> 119 us
    all_to_all x3 -> x0, blocking collectives: 294 us -> none  [moe_layer(): lax.all_to_all(outgoing, 'expert', split_axis=0, concat_axis=0, tiled=True)]
    ppermute x0 -> x45, waiting for transfers between devices: none -> 209 us  [pairwise_exchange(): lax.ppermute(sent, axis, [(i, i ^ hop) for i in range(peers)])]
    ppermute x0 -> x45, starting transfers between devices: none -> 87.8 us  [pairwise_exchange(): lax.ppermute(sent, axis, [(i, i ^ hop) for i in range(peers)])]
    unnamed x22 -> x88, local copies, waits for them, and re-layouts: 1.53 us -> 34.6 us
    gather x0 -> x3, local copies, waits for them, and re-layouts: none -> 15.3 us  [pairwise_exchange(): pieces = jnp.stack(gathered)[index ^ jnp.arange(peers)]]
  transfers between devices with their start and end apart: 6 -> 51, of which waited for: 5 -> 36; matrix products, arithmetic and copies ran while one was open for 4% -> 10% of each run, Pallas kernels for 0% -> 0%
where the time goes in v1:
time: 876 us; the launch traced here: 869 us
  waiting for transfers between devices  472 us (54%)
  local copies, waits for them, and re-layouts  119 us (14%)
  starting transfers between devices  113 us (13%)
  blocking collectives  105 us (12%)
  other arithmetic  33.1 us (4%)
  matrix products  26.7 us (3%)
    all_to_all x3, waiting for transfers between devices, moe_layer(): lax.all_to_all(outgoing, 'expert', split_axis=0, concat_axis=0, tiled=True)  261 us
    ppermute x45, waiting for transfers between devices, pairwise_exchange(): lax.ppermute(sent, axis, [(i, i ^ hop) for i in range(peers)])  209 us
    ppermute x45, starting transfers between devices, pairwise_exchange(): lax.ppermute(sent, axis, [(i, i ^ hop) for i in range(peers)])  87.8 us
    all_gather x1, blocking collectives, local(): lax.all_gather(query_vectors, ('segment', 'expert'), axis=0, tiled=True)  59.8 us
    unnamed x1, blocking collectives  44.7 us
    unnamed x88, local copies, waits for them, and re-layouts  34.6 us
    gather x3, local copies, waits for them, and re-layouts, moe_layer(): returned.reshape(expert_count * capacity, model_width)[target]  24 us
    all_to_all x3, starting transfers between devices, moe_layer(): lax.all_to_all(outgoing, 'expert', split_axis=0, concat_axis=0, tiled=True)  20.2 us
  transfers between devices with their start and end apart: 51, of which 36 were waited for; matrix products, arithmetic and copies ran while one was open for 10% of the time, Pallas kernels for 0%

profile of v1, /device:TPU:14, one launch (start us, length us, event | category | flops | bytes accessed | tf_op | source)
XLA Modules:
  0.0 869.4 jit_solution(2379078438438628869)
XLA Ops:
  7.1 6.2 scatter_custom_fusion
  13.3 7.9 all-to-all-start
  30.7 84.8 %all-to-all-done = bf16[16,64,2048]{2,1,0:T(8,128)(2,1)} async-done(((bf16[16,64,2048]{2,1,0:T(8,128)(2,1)}), bf16[16,64,2048]{2,1,0:T(8,128)(2,1)}, u32[]{:S(2)}, u32[]{:S(2)}) %all-to-all-start) | async-done | bytes 4194336 | tf_op jit(solution)/shard_map/all_to_all | solution.py:80
  136.1 6.4 collective-permute-done.1
  149.9 9.2 %collective-permute-start.9 = (bf16[1,64,2048]{2,1,0:T(8,128)(2,1)}, bf16[1,64,2048]{2,1,0:T(8,128)(2,1)S(1)}, u32[]{:S(2)}, u32[]{:S(2)}) collective-permute-start(bf16[1,64,2048]{2,1,0:T(8,128)(2,1)} %get-tuple-element.56), channel_id=1, source_target_pairs={{0,10},{1,11},{2,8},{3,9},{4,14},{5,15},{6,12},{7,13},{8,2},{9,3},... | collective-permute-start | bytes 786440 | tf_op jit(solution)/shard_map/ppermute | solution.py:29
  159.8 6.7 collective-permute-start.10
  169.1 27.4 %collective-permute-done.8 = bf16[1,64,2048]{2,1,0:T(8,128)(2,1)S(1)} collective-permute-done((bf16[1,64,2048]{2,1,0:T(8,128)(2,1)}, bf16[1,64,2048]{2,1,0:T(8,128)(2,1)S(1)}, u32[]{:S(2)}, u32[]{:S(2)}) %collective-permute-start.8) | collective-permute-done | bytes 262176 | tf_op jit(solution)/shard_map/ppermute | solution.py:29
  196.4 8.5 collective-permute-start.13
  206.6 10.5 %collective-permute-done.10 = bf16[1,64,2048]{2,1,0:T(8,128)(2,1)S(1)} collective-permute-done((bf16[1,64,2048]{2,1,0:T(8,128)(2,1)}, bf16[1,64,2048]{2,1,0:T(8,128)(2,1)S(1)}, u32[]{:S(2)}, u32[]{:S(2)}) %collective-permute-start.10) | collective-permute-done | bytes 262176 | tf_op jit(solution)/shard_map/ppermute | solution.py:29
  217.9 7.9 collective-permute-done.11
  229.1 7.8 collective-permute-done.13
  244.4 8.0 gather_fusion.1
  262.2 6.3 scatter_custom_fusion.1
  282.5 88.1 %all-to-all-done.1 = bf16[16,64,2048]{2,1,0:T(8,128)(2,1)} async-done(((bf16[16,64,2048]{2,1,0:T(8,128)(2,1)}), bf16[16,64,2048]{2,1,0:T(8,128)(2,1)}, u32[]{:S(2)}, u32[]{:S(2)}) %all-to-all-start.1) | async-done | bytes 4194336 | tf_op jit(solution)/shard_map/all_to_all | solution.py:80
  411.8 6.9 collective-permute-start.26
  422.1 22.9 %collective-permute-done.24 = bf16[1,64,2048]{2,1,0:T(8,128)(2,1)S(1)} collective-permute-done((bf16[1,64,2048]{2,1,0:T(8,128)(2,1)}, bf16[1,64,2048]{2,1,0:T(8,128)(2,1)S(1)}, u32[]{:S(2)}, u32[]{:S(2)}) %collective-permute-start.24) | collective-permute-done | bytes 262176 | tf_op jit(solution)/shard_map/ppermute | solution.py:29
  457.0 7.8 collective-permute-done.26
  465.5 10.5 %collective-permute-done.27 = bf16[1,64,2048]{2,1,0:T(8,128)(2,1)S(1)} collective-permute-done((bf16[1,64,2048]{2,1,0:T(8,128)(2,1)}, bf16[1,64,2048]{2,1,0:T(8,128)(2,1)S(1)}, u32[]{:S(2)}, u32[]{:S(2)}) %collective-permute-start.27) | collective-permute-done | bytes 262176 | tf_op jit(solution)/shard_map/ppermute | solution.py:29
  480.6 9.3 %collective-permute-done.29 = bf16[1,64,2048]{2,1,0:T(8,128)(2,1)S(1)} collective-permute-done((bf16[1,64,2048]{2,1,0:T(8,128)(2,1)S(1)}, bf16[1,64,2048]{2,1,0:T(8,128)(2,1)S(1)}, u32[]{:S(2)}, u32[]{:S(2)}) %collective-permute-start.29) | collective-permute-done | bytes 262176 | tf_op jit(solution)/shard_map/ppermute | solution.py:29
  496.5 8.0 gather_fusion.3
  513.5 6.6 scatter_custom_fusion.2
  533.2 88.5 %all-to-all-done.2 = bf16[16,64,2048]{2,1,0:T(8,128)(2,1)} async-done(((bf16[16,64,2048]{2,1,0:T(8,128)(2,1)}), bf16[16,64,2048]{2,1,0:T(8,128)(2,1)}, u32[]{:S(2)}, u32[]{:S(2)}) %all-to-all-start.2) | async-done | bytes 4194336 | tf_op jit(solution)/shard_map/all_to_all | solution.py:80
  658.6 7.1 collective-permute-start.42
  671.6 13.7 %collective-permute-done.40 = bf16[1,64,2048]{2,1,0:T(8,128)(2,1)S(1)} collective-permute-done((bf16[1,64,2048]{2,1,0:T(8,128)(2,1)}, bf16[1,64,2048]{2,1,0:T(8,128)(2,1)S(1)}, u32[]{:S(2)}, u32[]{:S(2)}) %collective-permute-start.40) | collective-permute-done | bytes 262176 | tf_op jit(solution)/shard_map/ppermute | solution.py:29
  688.8 7.7 collective-permute-done.41
  700.2 8.3 collective-permute-done.42
  709.3 11.9 %collective-permute-done.43 = bf16[1,64,2048]{2,1,0:T(8,128)(2,1)S(1)} collective-permute-done((bf16[1,64,2048]{2,1,0:T(8,128)(2,1)}, bf16[1,64,2048]{2,1,0:T(8,128)(2,1)S(1)}, u32[]{:S(2)}, u32[]{:S(2)}) %collective-permute-start.43) | collective-permute-done | bytes 262176 | tf_op jit(solution)/shard_map/ppermute | solution.py:29
  721.9 6.9 collective-permute-done.44
  729.5 6.9 collective-permute-done.45
  748.5 8.0 gather_fusion.5
  761.9 59.8 %all-gather = bf16[32,2,2048]{2,1,0:T(2,128)(2,1)S(1)} all-gather(bf16[1,2,2048]{2,1,0:T(2,128)(2,1)S(1)} %slice_bitcast_fusion), channel_id=1, replica_groups=mesh['segment'=2,'expert'=16] {'segment','expert'}, dimensions={0}, use_global_device_ids=true | all-gather | bytes 270336 | tf_op jit(solution)/shard_map/all_gather | solution.py:135
  823.7 44.7 %all-reduce.2 = (f32[64]{0:T(128)S(1)}, f32[64]{0:T(128)S(1)}) all-reduce(f32[64]{0:T(128)S(1)} %get-tuple-element.4, f32[64]{0:T(128)S(1)} %get-tuple-element.3), channel_id=3, replica_groups=mesh['segment'=2,'expert'=16] {'segment','expert'}, use_global_device_ids=true, to_apply=%region_27.29.clone | all-reduce | flops 128 | bytes 1024
  (278 shorter events, 246.6 us)
Async XLA Ops:
  13.3 102.2 %all-to-all-start = ((bf16[16,64,2048]{2,1,0:T(8,128)(2,1)}), bf16[16,64,2048]{2,1,0:T(8,128)(2,1)}, u32[]{:S(2)}, u32[]{:S(2)}) async-start(bf16[16,64,2048]{2,1,0:T(8,128)(2,1)} %bitcast.399), calls=%async_computation | async-start | bytes 8388608 | tf_op jit(solution)/shard_map/all_to_all | solution.py:80
  134.4 25.4 %collective-permute-start.5 = (bf16[1,64,2048]{2,1,0:T(8,128)(2,1)}, bf16[1,64,2048]{2,1,0:T(8,128)(2,1)S(1)}, u32[]{:S(2)}, u32[]{:S(2)}) collective-permute-start(bf16[1,64,2048]{2,1,0:T(8,128)(2,1)} %get-tuple-element.60), channel_id=1, source_target_pairs={{0,6},{1,7},{2,4},{3,5},{4,2},{5,3},{6,0},{7,1},{8,14},{9,15},{10,... | collective-permute-start | bytes 786440 | tf_op jit(solution)/shard_map/ppermute | solution.py:29
  142.4 24.7 %collective-permute-start.6 = (bf16[1,64,2048]{2,1,0:T(8,128)(2,1)}, bf16[1,64,2048]{2,1,0:T(8,128)(2,1)S(1)}, u32[]{:S(2)}, u32[]{:S(2)}) collective-permute-start(bf16[1,64,2048]{2,1,0:T(8,128)(2,1)} %get-tuple-element.59), channel_id=1, source_target_pairs={{0,7},{1,6},{2,5},{3,4},{4,3},{5,2},{6,1},{7,0},{8,15},{9,14},{10,... | collective-permute-start | bytes 786440 | tf_op jit(solution)/shard_map/ppermute | solution.py:29
  143.2 24.7 %collective-permute-start.7 = (bf16[1,64,2048]{2,1,0:T(8,128)(2,1)}, bf16[1,64,2048]{2,1,0:T(8,128)(2,1)S(1)}, u32[]{:S(2)}, u32[]{:S(2)}) collective-permute-start(bf16[1,64,2048]{2,1,0:T(8,128)(2,1)} %get-tuple-element.58), channel_id=1, source_target_pairs={{0,8},{1,9},{2,10},{3,11},{4,12},{5,13},{6,14},{7,15},{8,0},{9,1},... | collective-permute-start | bytes 786440 | tf_op jit(solution)/shard_map/ppermute | solution.py:29
  148.0 48.5 %collective-permute-start.8 = (bf16[1,64,2048]{2,1,0:T(8,128)(2,1)}, bf16[1,64,2048]{2,1,0:T(8,128)(2,1)S(1)}, u32[]{:S(2)}, u32[]{:S(2)}) collective-permute-start(bf16[1,64,2048]{2,1,0:T(8,128)(2,1)} %get-tuple-element.57), channel_id=1, source_target_pairs={{0,9},{1,8},{2,11},{3,10},{4,13},{5,12},{6,15},{7,14},{8,1},{9,0},... | collective-permute-start | bytes 786440 | tf_op jit(solution)/shard_map/ppermute | solution.py:29
  149.9 56.0 %collective-permute-start.9 = (bf16[1,64,2048]{2,1,0:T(8,128)(2,1)}, bf16[1,64,2048]{2,1,0:T(8,128)(2,1)S(1)}, u32[]{:S(2)}, u32[]{:S(2)}) collective-permute-start(bf16[1,64,2048]{2,1,0:T(8,128)(2,1)} %get-tuple-element.56), channel_id=1, source_target_pairs={{0,10},{1,11},{2,8},{3,9},{4,14},{5,15},{6,12},{7,13},{8,2},{9,3},... | collective-permute-start | bytes 786440 | tf_op jit(solution)/shard_map/ppermute | solution.py:29
  159.8 57.3 %collective-permute-start.10 = (bf16[1,64,2048]{2,1,0:T(8,128)(2,1)}, bf16[1,64,2048]{2,1,0:T(8,128)(2,1)S(1)}, u32[]{:S(2)}, u32[]{:S(2)}) collective-permute-start(bf16[1,64,2048]{2,1,0:T(8,128)(2,1)} %get-tuple-element.55), channel_id=1, source_target_pairs={{0,11},{1,10},{2,9},{3,8},{4,15},{5,14},{6,13},{7,12},{8,3},{9,2},... | collective-permute-start | bytes 786440 | tf_op jit(solution)/shard_map/ppermute | solution.py:29
  167.2 58.6 %collective-permute-start.11 = (bf16[1,64,2048]{2,1,0:T(8,128)(2,1)}, bf16[1,64,2048]{2,1,0:T(8,128)(2,1)S(1)}, u32[]{:S(2)}, u32[]{:S(2)}) collective-permute-start(bf16[1,64,2048]{2,1,0:T(8,128)(2,1)} %get-tuple-element.54), channel_id=1, source_target_pairs={{0,12},{1,13},{2,14},{3,15},{4,8},{5,9},{6,10},{7,11},{8,4},{9,5},... | collective-permute-start | bytes 786440 | tf_op jit(solution)/shard_map/ppermute | solution.py:29
  167.9 60.5 %collective-permute-start.12 = (bf16[1,64,2048]{2,1,0:T(8,128)(2,1)}, bf16[1,64,2048]{2,1,0:T(8,128)(2,1)S(1)}, u32[]{:S(2)}, u32[]{:S(2)}) collective-permute-start(bf16[1,64,2048]{2,1,0:T(8,128)(2,1)} %get-tuple-element.53), channel_id=1, source_target_pairs={{0,13},{1,12},{2,15},{3,14},{4,9},{5,8},{6,11},{7,10},{8,5},{9,4},... | collective-permute-start | bytes 786440 | tf_op jit(solution)/shard_map/ppermute | solution.py:29
  196.4 40.4 %collective-permute-start.13 = (bf16[1,64,2048]{2,1,0:T(8,128)(2,1)S(1)}, bf16[1,64,2048]{2,1,0:T(8,128)(2,1)S(1)}, u32[]{:S(2)}, u32[]{:S(2)}) collective-permute-start(bf16[1,64,2048]{2,1,0:T(8,128)(2,1)S(1)} %copy-done.6), channel_id=1, source_target_pairs={{0,14},{1,15},{2,12},{3,13},{4,10},{5,11},{6,8},{7,9},{8,6},{9,7},... | collective-permute-start | bytes 786440 | tf_op jit(solution)/shard_map/ppermute | solution.py:29
  205.9 32.7 %collective-permute-start.14 = (bf16[1,64,2048]{2,1,0:T(8,128)(2,1)S(1)}, bf16[1,64,2048]{2,1,0:T(8,128)(2,1)S(1)}, u32[]{:S(2)}, u32[]{:S(2)}) collective-permute-start(bf16[1,64,2048]{2,1,0:T(8,128)(2,1)S(1)} %get-tuple-element.51), channel_id=1, source_target_pairs={{0,15},{1,14},{2,13},{3,12},{4,11},{5,10},{6,9},{7,8},{8,7},{9,6},... | collective-permute-start | bytes 786440 | tf_op jit(solution)/shard_map/ppermute | solution.py:29
  268.5 102.1 %all-to-all-start.1 = ((bf16[16,64,2048]{2,1,0:T(8,128)(2,1)}), bf16[16,64,2048]{2,1,0:T(8,128)(2,1)}, u32[]{:S(2)}, u32[]{:S(2)}) async-start(bf16[16,64,2048]{2,1,0:T(8,128)(2,1)} %bitcast.401), calls=%async_computation.1 | async-start | bytes 8388608 | tf_op jit(solution)/shard_map/all_to_all | solution.py:80
  390.8 21.0 %collective-permute-start.21 = (bf16[1,64,2048]{2,1,0:T(8,128)(2,1)}, bf16[1,64,2048]{2,1,0:T(8,128)(2,1)S(1)}, u32[]{:S(2)}, u32[]{:S(2)}) collective-permute-start(bf16[1,64,2048]{2,1,0:T(8,128)(2,1)} %get-tuple-element.44), channel_id=1, source_target_pairs={{0,6},{1,7},{2,4},{3,5},{4,2},{5,3},{6,0},{7,1},{8,14},{9,15},{10,... | collective-permute-start | bytes 786440 | tf_op jit(solution)/shard_map/ppermute | solution.py:29
  394.2 25.1 %collective-permute-start.22 = (bf16[1,64,2048]{2,1,0:T(8,128)(2,1)}, bf16[1,64,2048]{2,1,0:T(8,128)(2,1)S(1)}, u32[]{:S(2)}, u32[]{:S(2)}) collective-permute-start(bf16[1,64,2048]{2,1,0:T(8,128)(2,1)} %get-tuple-element.43), channel_id=1, source_target_pairs={{0,7},{1,6},{2,5},{3,4},{4,3},{5,2},{6,1},{7,0},{8,15},{9,14},{10,... | collective-permute-start | bytes 786440 | tf_op jit(solution)/shard_map/ppermute | solution.py:29
  395.3 24.8 %collective-permute-start.23 = (bf16[1,64,2048]{2,1,0:T(8,128)(2,1)}, bf16[1,64,2048]{2,1,0:T(8,128)(2,1)S(1)}, u32[]{:S(2)}, u32[]{:S(2)}) collective-permute-start(bf16[1,64,2048]{2,1,0:T(8,128)(2,1)} %get-tuple-element.42), channel_id=1, source_target_pairs={{0,8},{1,9},{2,10},{3,11},{4,12},{5,13},{6,14},{7,15},{8,0},{9,1},... | collective-permute-start | bytes 786440 | tf_op jit(solution)/shard_map/ppermute | solution.py:29
  399.4 45.6 %collective-permute-start.24 = (bf16[1,64,2048]{2,1,0:T(8,128)(2,1)}, bf16[1,64,2048]{2,1,0:T(8,128)(2,1)S(1)}, u32[]{:S(2)}, u32[]{:S(2)}) collective-permute-start(bf16[1,64,2048]{2,1,0:T(8,128)(2,1)} %get-tuple-element.41), channel_id=1, source_target_pairs={{0,9},{1,8},{2,11},{3,10},{4,13},{5,12},{6,15},{7,14},{8,1},{9,0},... | collective-permute-start | bytes 786440 | tf_op jit(solution)/shard_map/ppermute | solution.py:29
  402.6 53.7 %collective-permute-start.25 = (bf16[1,64,2048]{2,1,0:T(8,128)(2,1)}, bf16[1,64,2048]{2,1,0:T(8,128)(2,1)S(1)}, u32[]{:S(2)}, u32[]{:S(2)}) collective-permute-start(bf16[1,64,2048]{2,1,0:T(8,128)(2,1)} %get-tuple-element.40), channel_id=1, source_target_pairs={{0,10},{1,11},{2,8},{3,9},{4,14},{5,15},{6,12},{7,13},{8,2},{9,3},... | collective-permute-start | bytes 786440 | tf_op jit(solution)/shard_map/ppermute | solution.py:29
  411.8 53.0 %collective-permute-start.26 = (bf16[1,64,2048]{2,1,0:T(8,128)(2,1)}, bf16[1,64,2048]{2,1,0:T(8,128)(2,1)S(1)}, u32[]{:S(2)}, u32[]{:S(2)}) collective-permute-start(bf16[1,64,2048]{2,1,0:T(8,128)(2,1)} %get-tuple-element.39), channel_id=1, source_target_pairs={{0,11},{1,10},{2,9},{3,8},{4,15},{5,14},{6,13},{7,12},{8,3},{9,2},... | collective-permute-start | bytes 786440 | tf_op jit(solution)/shard_map/ppermute | solution.py:29
  419.4 56.6 %collective-permute-start.27 = (bf16[1,64,2048]{2,1,0:T(8,128)(2,1)}, bf16[1,64,2048]{2,1,0:T(8,128)(2,1)S(1)}, u32[]{:S(2)}, u32[]{:S(2)}) collective-permute-start(bf16[1,64,2048]{2,1,0:T(8,128)(2,1)} %get-tuple-element.38), channel_id=1, source_target_pairs={{0,12},{1,13},{2,14},{3,15},{4,8},{5,9},{6,10},{7,11},{8,4},{9,5},... | collective-permute-start | bytes 786440 | tf_op jit(solution)/shard_map/ppermute | solution.py:29
  420.1 59.8 %collective-permute-start.28 = (bf16[1,64,2048]{2,1,0:T(8,128)(2,1)}, bf16[1,64,2048]{2,1,0:T(8,128)(2,1)S(1)}, u32[]{:S(2)}, u32[]{:S(2)}) collective-permute-start(bf16[1,64,2048]{2,1,0:T(8,128)(2,1)} %get-tuple-element.37), channel_id=1, source_target_pairs={{0,13},{1,12},{2,15},{3,14},{4,9},{5,8},{6,11},{7,10},{8,5},{9,4},... | collective-permute-start | bytes 786440 | tf_op jit(solution)/shard_map/ppermute | solution.py:29
  445.0 44.9 %collective-permute-start.29 = (bf16[1,64,2048]{2,1,0:T(8,128)(2,1)S(1)}, bf16[1,64,2048]{2,1,0:T(8,128)(2,1)S(1)}, u32[]{:S(2)}, u32[]{:S(2)}) collective-permute-start(bf16[1,64,2048]{2,1,0:T(8,128)(2,1)S(1)} %copy-done.7), channel_id=1, source_target_pairs={{0,14},{1,15},{2,12},{3,13},{4,10},{5,11},{6,8},{7,9},{8,6},{9,7},... | collective-permute-start | bytes 786440 | tf_op jit(solution)/shard_map/ppermute | solution.py:29
  456.2 34.4 %collective-permute-start.30 = (bf16[1,64,2048]{2,1,0:T(8,128)(2,1)S(1)}, bf16[1,64,2048]{2,1,0:T(8,128)(2,1)S(1)}, u32[]{:S(2)}, u32[]{:S(2)}) collective-permute-start(bf16[1,64,2048]{2,1,0:T(8,128)(2,1)S(1)} %get-tuple-element.35), channel_id=1, source_target_pairs={{0,15},{1,14},{2,13},{3,12},{4,11},{5,10},{6,9},{7,8},{8,7},{9,6},... | collective-permute-start | bytes 786440 | tf_op jit(solution)/shard_map/ppermute | solution.py:29
  520.2 101.6 %all-to-all-start.2 = ((bf16[16,64,2048]{2,1,0:T(8,128)(2,1)}), bf16[16,64,2048]{2,1,0:T(8,128)(2,1)}, u32[]{:S(2)}, u32[]{:S(2)}) async-start(bf16[16,64,2048]{2,1,0:T(8,128)(2,1)} %bitcast.400), calls=%async_computation.2 | async-start | bytes 8388608 | tf_op jit(solution)/shard_map/all_to_all | solution.py:80
  526.8 233.2 %collective-permute-start.31 = (bf16[64,2048]{1,0:T(8,128)(2,1)}, bf16[64,2048]{1,0:T(8,128)(2,1)}, u32[]{:S(2)}, u32[]{:S(2)}) collective-permute-start(bf16[64,2048]{1,0:T(8,128)(2,1)} %fusion.45), channel_id=1, source_target_pairs={{16,0},{17,1},{18,2},{19,3},{20,4},{21,5},{22,6},{23,7},{24,8},{25... | collective-permute-start | bytes 786440 | tf_op jit(solution)/shard_map/ppermute | solution.py:37
  650.7 34.6 %collective-permute-start.40 = (bf16[1,64,2048]{2,1,0:T(8,128)(2,1)}, bf16[1,64,2048]{2,1,0:T(8,128)(2,1)S(1)}, u32[]{:S(2)}, u32[]{:S(2)}) collective-permute-start(bf16[1,64,2048]{2,1,0:T(8,128)(2,1)} %get-tuple-element.26), channel_id=1, source_target_pairs={{0,8},{1,9},{2,10},{3,11},{4,12},{5,13},{6,14},{7,15},{8,0},{9,1},... | collective-permute-start | bytes 786440 | tf_op jit(solution)/shard_map/ppermute | solution.py:29
  654.4 42.1 %collective-permute-start.41 = (bf16[1,64,2048]{2,1,0:T(8,128)(2,1)}, bf16[1,64,2048]{2,1,0:T(8,128)(2,1)S(1)}, u32[]{:S(2)}, u32[]{:S(2)}) collective-permute-start(bf16[1,64,2048]{2,1,0:T(8,128)(2,1)} %get-tuple-element.25), channel_id=1, source_target_pairs={{0,9},{1,8},{2,11},{3,10},{4,13},{5,12},{6,15},{7,14},{8,1},{9,0},... | collective-permute-start | bytes 786440 | tf_op jit(solution)/shard_map/ppermute | solution.py:29
  658.6 49.9 %collective-permute-start.42 = (bf16[1,64,2048]{2,1,0:T(8,128)(2,1)}, bf16[1,64,2048]{2,1,0:T(8,128)(2,1)S(1)}, u32[]{:S(2)}, u32[]{:S(2)}) collective-permute-start(bf16[1,64,2048]{2,1,0:T(8,128)(2,1)} %get-tuple-element.24), channel_id=1, source_target_pairs={{0,10},{1,11},{2,8},{3,9},{4,14},{5,15},{6,12},{7,13},{8,2},{9,3},... | collective-permute-start | bytes 786440 | tf_op jit(solution)/shard_map/ppermute | solution.py:29
  666.4 54.7 %collective-permute-start.43 = (bf16[1,64,2048]{2,1,0:T(8,128)(2,1)}, bf16[1,64,2048]{2,1,0:T(8,128)(2,1)S(1)}, u32[]{:S(2)}, u32[]{:S(2)}) collective-permute-start(bf16[1,64,2048]{2,1,0:T(8,128)(2,1)} %get-tuple-element.23), channel_id=1, source_target_pairs={{0,11},{1,10},{2,9},{3,8},{4,15},{5,14},{6,13},{7,12},{8,3},{9,2},... | collective-permute-start | bytes 786440 | tf_op jit(solution)/shard_map/ppermute | solution.py:29
  685.3 43.5 %collective-permute-start.44 = (bf16[1,64,2048]{2,1,0:T(8,128)(2,1)}, bf16[1,64,2048]{2,1,0:T(8,128)(2,1)S(1)}, u32[]{:S(2)}, u32[]{:S(2)}) collective-permute-start(bf16[1,64,2048]{2,1,0:T(8,128)(2,1)} %get-tuple-element.22), channel_id=1, source_target_pairs={{0,12},{1,13},{2,14},{3,15},{4,8},{5,9},{6,10},{7,11},{8,4},{9,5},... | collective-permute-start | bytes 786440 | tf_op jit(solution)/shard_map/ppermute | solution.py:29
  696.5 39.9 %collective-permute-start.45 = (bf16[1,64,2048]{2,1,0:T(8,128)(2,1)S(1)}, bf16[1,64,2048]{2,1,0:T(8,128)(2,1)S(1)}, u32[]{:S(2)}, u32[]{:S(2)}) collective-permute-start(bf16[1,64,2048]{2,1,0:T(8,128)(2,1)S(1)} %copy-done.5), channel_id=1, source_target_pairs={{0,13},{1,12},{2,15},{3,14},{4,9},{5,8},{6,11},{7,10},{8,5},{9,4},... | collective-permute-start | bytes 786440 | tf_op jit(solution)/shard_map/ppermute | solution.py:29
  708.5 31.4 %collective-permute-start.46 = (bf16[1,64,2048]{2,1,0:T(8,128)(2,1)S(1)}, bf16[1,64,2048]{2,1,0:T(8,128)(2,1)S(1)}, u32[]{:S(2)}, u32[]{:S(2)}) collective-permute-start(bf16[1,64,2048]{2,1,0:T(8,128)(2,1)S(1)} %copy-done.4), channel_id=1, source_target_pairs={{0,14},{1,15},{2,12},{3,13},{4,10},{5,11},{6,8},{7,9},{8,6},{9,7},... | collective-permute-start | bytes 786440 | tf_op jit(solution)/shard_map/ppermute | solution.py:29
  721.2 21.5 %collective-permute-start.47 = (bf16[1,64,2048]{2,1,0:T(8,128)(2,1)S(1)}, bf16[1,64,2048]{2,1,0:T(8,128)(2,1)S(1)}, u32[]{:S(2)}, u32[]{:S(2)}) collective-permute-start(bf16[1,64,2048]{2,1,0:T(8,128)(2,1)S(1)} %copy-done.3), channel_id=1, source_target_pairs={{0,15},{1,14},{2,13},{3,12},{4,11},{5,10},{6,9},{7,8},{8,7},{9,6},... | collective-permute-start | bytes 786440 | tf_op jit(solution)/shard_map/ppermute | solution.py:29
  (43 other events, 865.9 us)
